TPU v7x, 32 devices: a whole 2x2x4 slice. The times are simulated.
32 devices in a mesh: rep: 2 (over x), gx: 16 (over z, y, core).
Axes of the slice: x: 2, y: 2, z: 4, core: 2. Of those that a mesh axis runs over, the one named last changes fastest.
Arguments:
- first_tokens: bfloat16 [64, 18432], P('rep', 'gx'), parts along dimension 0, may hold values from -6 to 6
- second_tokens: bfloat16 [64, 18432], P('rep', 'gx'), parts along dimension 0, may hold values from -6 to 6
- ln_gain: bfloat16 [18432], P('gx'), may hold values from 0.099609375 to 1.8984375
- qkv_weight: bfloat16 [18432, 6656], P('gx')
- out_weight: bfloat16 [6144, 18432], P(None, 'gx'), may hold values from -0.078125 to 0.078125
- kv_cache: bfloat16 [64, 1024, 512], P(('rep', 'gx')), parts along dimension 0, as said below
- lengths: int32 [64], P(('rep', 'gx')), parts along dimension 0, may hold values from 256 to 1024, as said below
- order: int32 [64], P('rep'), parts along dimension 0, may hold values from 0 to 31, each once
Outputs:
- first_out: bfloat16 [64, 18432], P('rep', 'gx'), parts along dimension 0
- second_out: bfloat16 [64, 18432], P('rep', 'gx'), parts along dimension 0
There are 2 independent parts, one for each index of `rep`. A program takes and returns all parts, laid end to end along the dimension named above; an argument that names none is the same for every part. Nothing has to cross between parts.
Inputs may be any that keep to these rules, and one draw needn't show every extreme that they name: `lengths`: some slot has exactly 256 and some slot exactly 1024 cached positions. `kv_cache`: entries of key columns and value columns are finite; a request's key scale may differ from another's.
All inputs are finite; a program needn't handle non-finite values.
Results may differ from a plain program's by a relative error of at most 0.005.
The roundings to bfloat16 on the way count: a program that leaves them out, or rounds other values in their place, can miss the bound.
Values may be sent and summed in bfloat16 or wider, within the bound.
A program may use at most 128 MiB of HBM per device.

v0:
```python
import jax
import jax.numpy as jnp
from jax import lax
from jax.sharding import PartitionSpec as P

D = 18432
HEADS = 24
HD = 256


eps_norm = 1e-05


def rotate(vectors, positions):
    half_width = vectors.shape[-1] // 2
    frequencies = 10000.0 ** (-jnp.arange(half_width, dtype=jnp.float32) / half_width)
    angles = positions.astype(jnp.float32)[..., None] * frequencies
    cosines = jnp.cos(angles)
    sine_terms = jnp.sin(angles)
    lower_half = vectors[..., :half_width]
    upper_half = vectors[..., half_width:]
    return jnp.concatenate(
        [
            lower_half * cosines - upper_half * sine_terms,
            upper_half * cosines + lower_half * sine_terms,
        ],
        axis=-1,
    )


def moments(token_rows):
    widened = token_rows.astype(jnp.float32)
    return lax.psum((jnp.sum(widened, axis=1), jnp.sum(widened * widened, axis=1)), "gx")


def normalize(token_rows, gain, totals, squares):
    widened = token_rows.astype(jnp.float32)
    mean_value = totals / D
    variance = squares / D - mean_value * mean_value
    scaled = (widened - mean_value[:, None]) * lax.rsqrt(variance[:, None] + eps_norm)
    return (scaled * gain.astype(jnp.float32)).astype(jnp.bfloat16)


def project(slot_rows, weight):
    return lax.psum_scatter(
        jnp.dot(slot_rows, weight, preferred_element_type=jnp.float32),
        "gx",
        scatter_dimension=0,
        tiled=True,
    )


def mix_heads(heads, weight):
    return jnp.dot(
        lax.all_gather(heads, "gx", axis=0, tiled=True), weight, preferred_element_type=jnp.float32
    )


def split_heads(projected, positions):
    queries = projected[:, : HEADS * HD].reshape(projected.shape[0], HEADS, HD)
    queries = rotate(queries, positions[:, None]).astype(jnp.bfloat16)
    keys_new = rotate(projected[:, HEADS * HD : HEADS * HD + HD], positions).astype(jnp.bfloat16)
    values_new = projected[:, HEADS * HD + HD :].astype(jnp.bfloat16)
    return (queries, keys_new, values_new)


def attend(queries, kv_cache, lengths, keys_new, values_new):
    score_scale = HD ** (-0.5)
    scores_new = (
        jnp.einsum("rhd,rjd->rhj", queries, keys_new, preferred_element_type=jnp.float32)
        * score_scale
    )
    scores_old = (
        jnp.einsum("rhd,rcd->rhc", queries, kv_cache[:, :, :HD], preferred_element_type=jnp.float32)
        * score_scale
    )
    live_mask = jnp.arange(kv_cache.shape[1])[None, None, :] < lengths[:, None, None]
    scores_old = jnp.where(live_mask, scores_old, -jnp.inf)
    peak_score = jnp.maximum(jnp.max(scores_old, axis=2), jnp.max(scores_new, axis=2))
    weights_old = jnp.exp(scores_old - peak_score[..., None])
    denominator = jnp.sum(weights_old, axis=2)
    weighted = jnp.einsum(
        "rhc,rcd->rhd",
        weights_old.astype(jnp.bfloat16),
        kv_cache[:, :, HD:],
        preferred_element_type=jnp.float32,
    )
    weights_new = jnp.exp(scores_new - peak_score[..., None])
    denominator = denominator + jnp.sum(weights_new, axis=2)
    weighted = weighted + jnp.einsum(
        "rhj,rjd->rhd",
        weights_new.astype(jnp.bfloat16),
        values_new,
        preferred_element_type=jnp.float32,
    )
    return (weighted / denominator[..., None]).astype(jnp.bfloat16)


def on_device(
    first_tokens, second_tokens, ln_gain, qkv_weight, out_weight, kv_cache, lengths, order
):
    request_count = order.shape[0]
    local_slots = kv_cache.shape[0]
    inverse = (
        jnp.zeros((request_count,), jnp.int32)
        .at[order]
        .set(jnp.arange(request_count, dtype=jnp.int32))
    )
    first_totals, first_squares = moments(first_tokens)
    first_proj = project(
        normalize(first_tokens, ln_gain, first_totals, first_squares)[order], qkv_weight
    )
    second_totals, second_squares = moments(second_tokens)
    second_proj = project(
        normalize(second_tokens, ln_gain, second_totals, second_squares)[order], qkv_weight
    )
    first_q, first_k, first_v = split_heads(first_proj, lengths)
    second_q, second_k, second_v = split_heads(second_proj, lengths + 1)
    heads_one = attend(first_q, kv_cache, lengths, first_k[:, None], first_v[:, None]).reshape(
        local_slots, HEADS * HD
    )
    heads_two = attend(
        second_q,
        kv_cache,
        lengths,
        jnp.stack([first_k, second_k], 1),
        jnp.stack([first_v, second_v], 1),
    ).reshape(local_slots, HEADS * HD)
    first_mixed = mix_heads(heads_one, out_weight)
    second_mixed = mix_heads(heads_two, out_weight)
    first_out = (first_tokens.astype(jnp.float32) + first_mixed[inverse]).astype(jnp.bfloat16)
    second_out = (second_tokens.astype(jnp.float32) + second_mixed[inverse]).astype(jnp.bfloat16)
    return (first_out, second_out)


def solution(mesh):
    return jax.shard_map(
        on_device,
        mesh=mesh,
        in_specs=(
            P("rep", "gx"),
            P("rep", "gx"),
            P("gx"),
            P("gx", None),
            P(None, "gx"),
            P(("rep", "gx"), None, None),
            P(("rep", "gx")),
            P("rep"),
        ),
        out_specs=(P("rep", "gx"), P("rep", "gx")),
        check_vma=False,
    )
```

profile of v0, /device:TPU:0, one launch (start us, length us, event | category | flops | bytes accessed | tf_op | source)
XLA Modules:
  0.0 226.2 jit_solution(7662958572170022277)
XLA Ops:
  7.2 1.0 convert_reduce_fusion
  8.2 1.0 convert_reduce_fusion.1
  9.2 0.7 convert_element_type.77
  9.9 0.7 compare_select_fusion.1
  10.6 34.9 %all-reduce.2 = (f32[32]{0:T(128)S(1)}, f32[32]{0:T(128)S(1)}, f32[32]{0:T(128)S(1)}, f32[32]{0:T(128)S(1)}) all-reduce(f32[32]{0:T(128)S(1)} %get-tuple-element.5, f32[32]{0:T(128)S(1)} %get-tuple-element.4, f32[32]{0:T(128)S(1)} %get-tuple-element.3, f32[32]{0:T(128)S(1)} %get-tuple-element.2), channel_id=1, replica_groups=mesh['rep'=2,'gx'=16] {'gx'}, use_global_device_ids=true, to_apply=%region_3.0 | all-reduce | flops 128 | bytes 1024 | tf_op jit(solution)/shard_map/psum | solution.py:33
  45.5 1.0 fusion.21
  46.6 0.6 gather_fusion
  47.2 0.6 gather_fusion.2
  47.9 9.1 %fusion.61 = f32[32,6656]{1,0:T(8,128)} fusion(bf16[32,1152]{1,0:T(8,128)(2,1)S(1)} %gather_fusion, bf16[1152,6656]{1,0:T(8,128)(2,1)} %param.11), kind=kOutput, calls=%fused_computation.114 | convolution fusion | flops 490733568 | bytes 16261120 | tf_op jit(solution)/shard_map/dot_general | solution.py:46
  57.0 0.9 copy-done
  57.9 3.7 %fusion.63 = f32[32,6656]{1,0:T(8,128)} fusion(bf16[32,1152]{1,0:T(8,128)(2,1)S(1)} %gather_fusion.2, bf16[1152,6656]{1,0:T(8,128)(2,1)S(1)} %copy-done), kind=kOutput, calls=%fused_computation.116 | convolution fusion | flops 490733568 | bytes 16261120 | tf_op jit(solution)/shard_map/dot_general | solution.py:46
  62.8 0.7 scatter_custom_fusion
  63.7 91.1 %all-reduce.6.cloned.1.call-done = (f32[32,6656]{1,0:T(8,128)}, f32[32,6656]{1,0:T(8,128)}) async-done(((f32[32,6656]{1,0:T(8,128)}, f32[32,6656]{1,0:T(8,128)}), (f32[32,6656]{1,0:T(8,128)}, f32[32,6656]{1,0:T(8,128)})) %all-reduce.6.cloned.1.call-update) | async-done | bytes 1703952
  154.8 0.9 constant_dynamic-slice_fusion.1
  155.7 0.8 fusion.44
  156.5 0.8 fusion.57
  157.3 0.9 constant_dynamic-slice_fusion
  158.2 0.9 fusion.46
  160.6 21.2 %all-gather.1 = bf16[16,2,6144]{2,1,0:T(2,128)(2,1)S(1)} all-gather(bf16[1,2,6144]{2,1,0:T(2,128)(2,1)S(1)} %reshape.316), channel_id=1, replica_groups=mesh['rep'=2,'gx'=16] {'gx'}, dimensions={0}, use_global_device_ids=true | all-gather | bytes 417792 | tf_op jit(solution)/shard_map/all_gather | solution.py:55
  182.0 7.4 %fusion.64 = f32[32,1152]{1,0:T(8,128)S(1)} fusion(bf16[32,6144]{1,0:T(8,128)(2,1)S(1)} %reshape.317, bf16[6144,1152]{1,0:T(8,128)(2,1)} %param.12), kind=kOutput, calls=%fused_computation.117 | convolution fusion | flops 452984832 | bytes 14696448 | tf_op jit(solution)/shard_map/dot_general | solution.py:54
  190.1 0.7 fusion.23
  191.9 18.5 %all-gather = bf16[16,2,6144]{2,1,0:T(2,128)(2,1)S(1)} all-gather(bf16[1,2,6144]{2,1,0:T(2,128)(2,1)S(1)} %reshape.314), channel_id=1, replica_groups=mesh['rep'=2,'gx'=16] {'gx'}, dimensions={0}, use_global_device_ids=true | all-gather | bytes 417792 | tf_op jit(solution)/shard_map/all_gather | solution.py:55
  210.6 7.4 %fusion.62 = f32[32,1152]{1,0:T(8,128)S(1)} fusion(bf16[32,6144]{1,0:T(8,128)(2,1)S(1)} %reshape.315, bf16[6144,1152]{1,0:T(8,128)(2,1)} %param.12), kind=kOutput, calls=%fused_computation.115 | convolution fusion | flops 452984832 | bytes 14696448 | tf_op jit(solution)/shard_map/dot_general | solution.py:54
  218.7 0.7 fusion.18
  (53 shorter events, 4.9 us)
Async XLA Ops:
  7.2 147.6 %all-reduce.6.cloned.1.call-start = ((), (), s32[]{:S(2)}) async-start(), calls=%async_computation | async-start | bytes 3407872
  47.9 10.0 %copy-start = (bf16[1152,6656]{1,0:T(8,128)(2,1)S(1)}, bf16[1152,6656]{1,0:T(8,128)(2,1)}, u32[]{:S(2)}) copy-start(bf16[1152,6656]{1,0:T(8,128)(2,1)} %param.11) | copy-start | bytes 46006276
  57.9 3.7 %copy-start.5 = (u32[32]{0:T(128)S(1)}, u32[32]{0:T(128)}, u32[]{:S(2)}) copy-start(u32[32]{0:T(128)} %constant.31) | copy-start | bytes 388
  57.9 5.7 %copy-start.4 = (s32[2]{0:T(128)S(1)}, s32[2]{0:T(128)}, u32[]{:S(2)}) copy-start(s32[2]{0:T(128)} %param.14) | copy-start | bytes 28
  57.9 101.3 %copy-start.1 = (bf16[2,1024,512]{2,1,0:T(8,128)(2,1)S(1)}, bf16[2,1024,512]{2,1,0:T(8,128)(2,1)}, u32[]{:S(2)}) copy-start(bf16[2,1024,512]{2,1,0:T(8,128)(2,1)} %param.13) | copy-start | bytes 6291460
  61.6 128.5 %copy-start.2 = (bf16[32,1152]{1,0:T(8,128)(2,1)S(1)}, bf16[32,1152]{1,0:T(8,128)(2,1)}, u32[]{:S(2)}) copy-start(bf16[32,1152]{1,0:T(8,128)(2,1)} %param.9) | copy-start | bytes 221188
  190.1 28.6 %copy-start.3 = (bf16[32,1152]{1,0:T(8,128)(2,1)S(1)}, bf16[32,1152]{1,0:T(8,128)(2,1)}, u32[]{:S(2)}) copy-start(bf16[32,1152]{1,0:T(8,128)(2,1)} %param.8) | copy-start | bytes 221188
Sparse Core Ops, SparseCore 0:
  61.7 93.0 all-reduce.5
where the time goes:
time: 227 us; the launch traced here: 226 us
  waiting for transfers between devices  91.1 us (40%)
  blocking collectives  74.7 us (33%)
  matrix products  29.7 us (13%)
  between operations  15 us (7%)
  other arithmetic  7.99 us (4%)
  local copies, waits for them, and re-layouts  7.76 us (3%)
    unnamed x2, waiting for transfers between devices  91.1 us
    all_gather x2, blocking collectives, mix_heads(): lax.all_gather(heads, 'gx', axis=0, tiled=True)  39.8 us
    psum x1, blocking collectives, moments(): lax.psum((jnp.sum(widened, axis=1), jnp.sum(widened * widened, axis=1)),...  34.9 us
    dot_general x2, matrix products, mix_heads(): jnp.dot(lax.all_gather(heads, 'gx', axis=0, tiled=True), weight, preferre...  14.8 us
    dot_general x2, matrix products, project(): jnp.dot(slot_rows, weight, preferred_element_type=jnp.float32)  12.8 us
  transfers between devices with their start and end apart: 1, of which 1 were waited for; matrix products, arithmetic and copies ran while one was open for 1% of the time, Pallas kernels for 0%

commit v1 on v0

v1 whole, which is shorter than its diff:
```python
import functools

import jax
import jax.numpy as jnp
import numpy as np
from jax import lax
from jax.experimental import pallas as pl
from jax.experimental.pallas import tpu as pltpu
from jax.sharding import PartitionSpec as P

D = 18432
HEADS = 24
HD = 256
HALF = HD // 2
KV = 2 * HD

GROUP = 8
GROUPS = HEADS // GROUP
TILE = 512

eps_norm = 1e-05

F32 = jnp.float32
BF16 = jnp.bfloat16


def dot_nt(a, b):
    return lax.dot_general(a, b, (((1,), (1,)), ((), ())), preferred_element_type=F32)


def dot_nn(a, b):
    return jnp.dot(a, b, preferred_element_type=F32)


def chunk_columns(j):
    width = GROUP * HD
    return (0, KV + width) if j == 0 else (KV + j * width, width)


def kernel(
    n,
    slots,
    first_ref,
    second_ref,
    gain_ref,
    freq_ref,
    qkv_ref,
    out_w_ref,
    cache_ref,
    lengths_ref,
    order_ref,
    first_out_ref,
    second_out_ref,
    x,
    wq,
    wo,
    cache,
    stat_own,
    stat_in,
    normed,
    partial,
    from_core,
    from_mid,
    from_hi,
    query,
    new_kv,
    gathered,
    spread,
    lhs,
    total,
    in_sem,
    q_sem,
    o_sem,
    stat_send,
    stat_recv,
    core_send,
    core_recv,
    mid_send,
    mid_recv,
    hi_send,
    hi_recv,
    ghi_send,
    ghi_recv,
    gmid_send,
    gmid_recv,
    gcore_send,
    gcore_recv,
):
    H = n // 4
    R = order_ref.shape[0]
    N = 2 * R
    rp = 2 * slots
    me = lax.axis_index("gx")
    core, mid, hi = me % 2, (me // 2) % 2, me // 4

    def index_of(hi_at, mid_at, core_at):
        return (hi_at * 2 + mid_at) * 2 + core_at

    sibling = index_of(hi, mid, 1 - core)
    across = index_of(hi, 1 - mid, core)
    ahead = [lax.rem(hi + d, H) for d in range(H)]
    behind = [lax.rem(hi - d + H, H) for d in range(H)]

    loads = [
        pltpu.make_async_copy(first_ref, x.at[pl.ds(0, R)], in_sem.at[0]),
        pltpu.make_async_copy(second_ref, x.at[pl.ds(R, R)], in_sem.at[1]),
    ]
    width = GROUP * HD
    kv_load = pltpu.make_async_copy(
        qkv_ref.at[:, pl.ds(HEADS * HD, KV)], wq.at[:, pl.ds(0, KV)], q_sem.at[GROUPS]
    )
    q_loads = [
        pltpu.make_async_copy(
            qkv_ref.at[:, pl.ds(j * width, width)],
            wq.at[:, pl.ds(KV + j * width, width)],
            q_sem.at[j],
        )
        for j in range(GROUPS)
    ]
    cache_load = pltpu.make_async_copy(cache_ref, cache, in_sem.at[2])
    o_loads = [
        pltpu.make_async_copy(
            out_w_ref.at[pl.ds(j * width, width)], wo.at[pl.ds(j * width, width)], o_sem.at[j]
        )
        for j in range(GROUPS)
    ]
    for copy in loads + [kv_load] + q_loads + [cache_load] + o_loads:
        copy.start()

    barrier = pltpu.get_barrier_semaphore()
    partners = [sibling, across] + [index_of(ahead[d], mid, core) for d in range(1, H)]
    for partner in partners:
        pl.semaphore_signal(
            barrier, inc=1, device_id={"gx": partner}, device_id_type=pl.DeviceIdType.MESH
        )

    sent = []

    def send(src, dst, send_sem, recv_sem, partner):
        copy = pltpu.make_async_remote_copy(
            src_ref=src,
            dst_ref=dst,
            send_sem=send_sem,
            recv_sem=recv_sem,
            device_id={"gx": partner},
            device_id_type=pl.DeviceIdType.MESH,
        )
        copy.start()
        sent.append(copy)
        return copy

    for copy in loads:
        copy.wait()
    rows = x[...]
    features = rows.shape[1]
    square = lax.broadcasted_iota(jnp.int32, (N, N), 0)
    across_lanes = lax.broadcasted_iota(jnp.int32, (N, N), 1)
    diagonal = square == across_lanes
    sums = dot_nt(jnp.ones((8, features), BF16), rows)
    squares = jnp.sum(jnp.where(diagonal, dot_nt(rows, rows), 0.0), axis=0, keepdims=True)
    line = lax.broadcasted_iota(jnp.int32, (8, N), 0)
    stat_own[...] = jnp.zeros_like(stat_own)
    stat_own[0, :, :N] = jnp.where(line == 0, sums, jnp.broadcast_to(squares, (8, N)))

    pl.semaphore_wait(barrier, len(partners))

    copy = send(stat_own.at[0], stat_in.at[0], stat_send.at[0], stat_recv.at[0], sibling)

    lane = lax.broadcasted_iota(jnp.int32, (8, N), 1)
    holder = jnp.zeros((8, N), jnp.int32)
    for p in range(R):
        device, slot = p // slots, p % slots
        at = (((device % 2) * 2 + (device // 2) % 2) * H + device // 4) * slots + slot
        holder = jnp.where(lane // 2 == at, order_ref[p], holder)
    holder = holder + (lane % 2) * R
    to_request = jnp.where(square == jnp.broadcast_to(holder[:1], (N, N)), 1.0, 0.0).astype(BF16)
    unit = jnp.where(diagonal, 1.0, 0.0).astype(BF16)
    to_slot = dot_nt(unit, to_request).astype(BF16)

    def rotation(count, per_row):
        row = lax.broadcasted_iota(jnp.int32, (count, HALF), 0)
        position = jnp.zeros((count, HALF), jnp.int32)
        for slot in range(slots):
            position = jnp.where(row // (2 * per_row) == slot, lengths_ref[slot], position)
        position = position + (row // per_row) % 2
        angles = position.astype(F32) * freq_ref[...]
        return jnp.cos(angles), jnp.sin(angles)

    q_cos, q_sin = rotation(rp * GROUP, GROUP)

    copy.wait_recv()
    stat_own[1] = stat_own[0] + stat_in[0]
    copy = send(stat_own.at[1], stat_in.at[1], stat_send.at[1], stat_recv.at[1], across)
    k_cos, k_sin = rotation(rp, 1)
    copy.wait_recv()
    stat_own[2] = stat_own[1] + stat_in[1]
    copies = [
        send(
            stat_own.at[2],
            stat_in.at[1 + d],
            stat_send.at[1 + d],
            stat_recv.at[1 + d],
            index_of(ahead[d], mid, core),
        )
        for d in range(1, H)
    ]
    for copy in copies:
        copy.wait_recv()
    stats = stat_own[2]
    for d in range(1, H):
        stats = stats + stat_in[1 + d]

    def as_column(row):
        return jnp.sum(
            jnp.where(diagonal, jnp.broadcast_to(row, (N, N)), 0.0), axis=1, keepdims=True
        )

    mean = as_column(stats[0:1, :N]) / D
    variance = as_column(stats[1:2, :N]) / D - mean * mean
    scaled = (rows.astype(F32) - mean) * lax.rsqrt(variance + eps_norm)
    by_request = (scaled * gain_ref[...].astype(F32)).astype(BF16)
    normed[...] = dot_nn(to_slot, by_request).astype(BF16)

    def project(j):
        start, count = chunk_columns(j)
        if j == 0:
            kv_load.wait()
        q_loads[j].wait()

        @pl.loop(0, count // TILE)
        def _(i):
            at = pl.ds(pl.multiple_of(start + i * TILE, TILE), TILE)
            product = dot_nn(normed[...], wq[:, at])
            for g in range(n):
                partial[g // (2 * H), (g // H) % 2, g % H, :, at] = product[
                    g * rp : (g + 1) * rp
                ]

        at = pl.ds(start, count)
        return send(
            partial.at[1 - core, :, :, :, at],
            from_core.at[:, :, :, at],
            core_send.at[j],
            core_recv.at[j],
            sibling,
        )

    def add_core(j, copy):
        start, count = chunk_columns(j)
        at = pl.ds(start, count)
        copy.wait_recv()
        from_core[1 - mid, :, :, at] = from_core[1 - mid, :, :, at] + partial[core, 1 - mid, :, :, at]
        copy = send(
            from_core.at[1 - mid, :, :, at],
            from_mid.at[:, :, at],
            mid_send.at[j],
            mid_recv.at[j],
            across,
        )
        from_core[mid, :, :, at] = from_core[mid, :, :, at] + partial[core, mid, :, :, at]
        return copy

    def add_mid(j, copy):
        start, count = chunk_columns(j)
        at = pl.ds(start, count)
        copy.wait_recv()
        from_mid[:, :, at] = from_mid[:, :, at] + from_core[mid, :, :, at]
        return [
            send(
                from_mid.at[ahead[d], :, at],
                from_hi.at[d - 1, :, at],
                hi_send.at[j, d - 1],
                hi_recv.at[j, d - 1],
                index_of(ahead[d], mid, core),
            )
            for d in range(1, H)
        ]

    def turn(lower, upper, cosines, sines):
        return jnp.concatenate(
            [lower * cosines - upper * sines, upper * cosines + lower * sines], axis=1
        )

    def attend(j, copies):
        start, count = chunk_columns(j)
        at = pl.ds(start, count)
        for copy in copies:
            copy.wait_recv()
        rows = from_mid[hi, :, at]
        for d in range(1, H):
            rows = rows + from_hi[d - 1, :, at]
        q_start = 0
        if j == 0:
            q_start = KV
            keys = turn(rows[:, :HALF], rows[:, HALF:HD], k_cos, k_sin)
            both = jnp.concatenate([keys, rows[:, HD:KV]], axis=1)
            at_row = lax.broadcasted_iota(jnp.int32, (128, KV), 0)
            for slot in range(slots):
                one = jnp.broadcast_to(both[2 * slot : 2 * slot + 1], (128, KV))
                two = jnp.broadcast_to(both[2 * slot + 1 : 2 * slot + 2], (128, KV))
                padded = jnp.where(at_row == 0, one, jnp.where(at_row == 1, two, 0.0))
                new_kv[slot] = padded.astype(BF16)
            cache_load.wait()
        for h in range(GROUP):
            for part in range(2):
                begin = q_start + h * HD + part * HALF
                query[part, pl.ds(h, rp, stride=GROUP), :] = rows[:, begin : begin + HALF]
        queries = turn(query[0], query[1], q_cos, q_sin)
        scale = HD ** (-0.5)
        context = cache.shape[1]
        span = 2 * GROUP
        lane_old = lax.broadcasted_iota(jnp.int32, (span, context), 1)
        lane_new = lax.broadcasted_iota(jnp.int32, (span, 128), 1)
        step = lax.broadcasted_iota(jnp.int32, (span, 128), 0) // GROUP
        results = []
        for slot in range(slots):
            q = queries[slot * span : (slot + 1) * span].astype(BF16)
            old = dot_nt(q, cache[slot, :, :HD]) * scale
            new = dot_nt(q, new_kv[slot, :, :HD]) * scale
            old = jnp.where(lane_old < lengths_ref[slot], old, -jnp.inf)
            new = jnp.where(lane_new <= step, new, -jnp.inf)
            peak = jnp.maximum(
                jnp.max(old, axis=1, keepdims=True), jnp.max(new, axis=1, keepdims=True)
            )
            old = jnp.exp(old - peak)
            new = jnp.exp(new - peak)
            denominator = jnp.sum(old, axis=1, keepdims=True) + jnp.sum(
                new, axis=1, keepdims=True
            )
            weighted = dot_nn(old.astype(BF16), cache[slot, :, HD:])
            weighted = weighted + dot_nn(new.astype(BF16), new_kv[slot, :, HD:])
            results.append(weighted / denominator)
        gathered[j, core, mid, hi] = jnp.concatenate(results, axis=0).astype(BF16)
        block = gathered.at[j, core, mid, hi]
        return [
            send(
                block,
                block,
                ghi_send.at[j, d - 1],
                ghi_recv.at[j, d - 1],
                index_of(ahead[d], mid, core),
            )
            for d in range(1, H)
        ]

    def pass_mid(j, copies):
        for copy in copies:
            copy.wait_recv()
        block = gathered.at[j, core, mid]
        return send(block, block, gmid_send.at[j], gmid_recv.at[j], across)

    def pass_core(j, copy):
        copy.wait_recv()
        block = gathered.at[j, core]
        return send(block, block, gcore_send.at[j], gcore_recv.at[j], sibling)

    def mix(j, copy):
        copy.wait_recv()
        o_loads[j].wait()
        everything = gathered[j].reshape(N * GROUP, HD).astype(F32)
        spread[0] = everything[:, :HALF]
        spread[1] = everything[:, HALF:]
        for h in range(GROUP):
            head = jnp.concatenate(
                [spread[part, pl.ds(h, N, stride=GROUP), :] for part in range(2)], axis=1
            ).astype(BF16)
            lhs[:, h * HD : (h + 1) * HD] = dot_nn(to_request, head).astype(BF16)

        for k in range(0, width, 512):
            product = dot_nn(lhs[:, k : k + 512], wo[j * width + k : j * width + k + 512, :])
            if j == 0 and k == 0:
                total[...] = product
            else:
                total[...] += product

    a0 = project(0)
    a1 = project(1)
    b0 = add_core(0, a0)
    a2 = project(2)
    b1 = add_core(1, a1)
    b2 = add_core(2, a2)
    c0 = add_mid(0, b0)
    c1 = add_mid(1, b1)
    g0 = attend(0, c0)
    c2 = add_mid(2, b2)
    g1 = attend(1, c1)
    g0 = pass_mid(0, g0)
    g2 = attend(2, c2)
    g1 = pass_mid(1, g1)
    g0 = pass_core(0, g0)
    g2 = pass_mid(2, g2)
    g1 = pass_core(1, g1)
    mix(0, g0)
    g2 = pass_core(2, g2)
    mix(1, g1)
    mix(2, g2)
    first_out_ref[...] = (x[:R].astype(F32) + total[:R]).astype(BF16)
    second_out_ref[...] = (x[R:].astype(F32) + total[R:]).astype(BF16)
    for copy in sent:
        copy.wait_send()


def on_device(
    n, first_tokens, second_tokens, ln_gain, qkv_weight, out_weight, kv_cache, lengths, order
):
    R, features = first_tokens.shape
    slots, context, _ = kv_cache.shape
    N, rp, H = 2 * R, 2 * slots, n // 4
    columns = qkv_weight.shape[1]
    lanes = max(N, 128)
    frequencies = (10000.0 ** (-np.arange(HALF) / HALF)).astype(np.float32)[None]
    anywhere = pl.BlockSpec(memory_space=pl.ANY)
    vmem = pl.BlockSpec(memory_space=pltpu.VMEM)
    smem = pl.BlockSpec(memory_space=pltpu.SMEM)
    dma = pltpu.SemaphoreType.DMA
    return pl.pallas_call(
        functools.partial(kernel, n, slots),
        out_shape=[jax.ShapeDtypeStruct((R, features), BF16)] * 2,
        in_specs=[anywhere, anywhere, vmem, vmem, anywhere, anywhere, anywhere, smem, smem],
        out_specs=[vmem, vmem],
        scratch_shapes=[
            pltpu.VMEM((N, features), BF16),
            pltpu.VMEM((features, columns), BF16),
            pltpu.VMEM((HEADS * HD, features), BF16),
            pltpu.VMEM((slots, context, KV), BF16),
            pltpu.VMEM((3, 8, lanes), F32),
            pltpu.VMEM((H + 1, 8, lanes), F32),
            pltpu.VMEM((N, features), BF16),
            pltpu.VMEM((2, 2, H, rp, columns), F32),
            pltpu.VMEM((2, H, rp, columns), F32),
            pltpu.VMEM((H, rp, columns), F32),
            pltpu.VMEM((H - 1, rp, columns), F32),
            pltpu.VMEM((2, rp * GROUP, HALF), F32),
            pltpu.VMEM((slots, 128, KV), BF16),
            pltpu.VMEM((GROUPS, 2, 2, H, rp * GROUP, HD), BF16),
            pltpu.VMEM((2, N * GROUP, HALF), F32),
            pltpu.VMEM((N, GROUP * HD), BF16),
            pltpu.VMEM((N, features), F32),
            dma((3,)),
            dma((GROUPS + 1,)),
            dma((GROUPS,)),
            dma((H + 1,)),
            dma((H + 1,)),
            dma((GROUPS,)),
            dma((GROUPS,)),
            dma((GROUPS,)),
            dma((GROUPS,)),
            dma((GROUPS, H - 1)),
            dma((GROUPS, H - 1)),
            dma((GROUPS, H - 1)),
            dma((GROUPS, H - 1)),
            dma((GROUPS,)),
            dma((GROUPS,)),
            dma((GROUPS,)),
            dma((GROUPS,)),
        ],
        compiler_params=pltpu.CompilerParams(
            collective_id=0, has_side_effects=True, vmem_limit_bytes=56 * 2**20
        ),
    )(
        first_tokens,
        second_tokens,
        ln_gain[None],
        jnp.asarray(frequencies),
        qkv_weight,
        out_weight,
        kv_cache,
        lengths,
        order,
    )


def solution(mesh):
    return jax.shard_map(
        functools.partial(on_device, mesh.shape["gx"]),
        mesh=mesh,
        in_specs=(
            P("rep", "gx"),
            P("rep", "gx"),
            P("gx"),
            P("gx", None),
            P(None, "gx"),
            P(("rep", "gx"), None, None),
            P(("rep", "gx")),
            P("rep"),
        ),
        out_specs=(P("rep", "gx"), P("rep", "gx")),
        check_vma=False,
    )
```

time: 227 us -> 55 us (0.24)
  waiting for transfers between devices: 91.1 us -> 0 us
  blocking collectives: 74.7 us -> 0 us
  Pallas kernels: 0 us -> 49.8 us
  matrix products: 29.7 us -> 0 us
  between operations: 15 us -> 0.64 us
  other arithmetic: 7.99 us -> 0 us
  local copies, waits for them, and re-layouts: 7.76 us -> 4.33 us
    unnamed x2 -> x0, waiting for transfers between devices: 91.1 us -> none
    pallas_call x0 -> x1, Pallas kernels: none -> 49.8 us  [on_device(): pl.pallas_call(functools.partial(kernel, n, slots), out_shape=[jax.ShapeD...]
    all_gather x2 -> x0, blocking collectives: 39.8 us -> none  [mix_heads(): lax.all_gather(heads, 'gx', axis=0, tiled=True)]
    psum x1 -> x0, blocking collectives: 34.9 us -> none  [moments(): lax.psum((jnp.sum(widened, axis=1), jnp.sum(widened * widened, axis=1)),...]
    dot_general x11 -> x0, matrix products: 29.7 us -> none  [the longest x2 14.8 us: mix_heads(): jnp.dot(lax.all_gather(heads, 'gx', axis=0, tiled=True), weight, preferre...]
    convert_element_type x5 -> x0, other arithmetic: 3.04 us -> none  [the longest x2 1.73 us: normalize(): return (scaled * gain.astype(jnp.float32)).astype(jnp.bfloat16)]
    gather x4 -> x0, local copies, waits for them, and re-layouts: 2.55 us -> none  [the longest x1 0.64 us: on_device(): normalize(first_tokens, ln_gain, first_totals, first_squares)[order]]
    reduce_sum x5 -> x0, other arithmetic: 2.43 us -> none  [the longest x2 2.03 us: moments(): jnp.sum(widened, axis=1)]
  transfers between devices with their start and end apart: 1 -> 0, of which waited for: 1 -> 0; matrix products, arithmetic and copies ran while one was open for 1% -> 0% of each run, Pallas kernels for 0% -> 0%
where the time goes in v1:
time: 55 us; the launch traced here: 54.7 us
  Pallas kernels  49.8 us (91%)
  local copies, waits for them, and re-layouts  4.33 us (8%)
  between operations  0.64 us (1%)
    pallas_call x1, Pallas kernels, on_device(): pl.pallas_call(functools.partial(kernel, n, slots), out_shape=[jax.ShapeD...  49.8 us
    unnamed x2, local copies, waits for them, and re-layouts  3.04 us
    broadcast_in_dim x1, local copies, waits for them, and re-layouts, on_device(): ln_gain[None]  1.28 us

profile of v1, /device:TPU:0, one launch (start us, length us, event | category | flops | bytes accessed | tf_op | source)
XLA Modules:
  0.0 54.7 jit_solution(12398458513570636316)
XLA Ops:
  0.6 1.3 %broadcast_in_dim.3.gain_ref = bf16[1,1152]{1,0:T(2,128)(2,1)} reshape(bf16[1152]{0:T(1024)(128)(2,1)} %param.11) | data formatting | bytes 4608 | tf_op jit(solution)/shard_map/broadcast_in_dim | solution.py:463
  1.9 49.8 %shard_map.104 = (bf16[32,1152]{1,0:T(8,128)(2,1)}, bf16[32,1152]{1,0:T(8,128)(2,1)}) custom-call(bf16[32,1152]{1,0:T(8,128)(2,1)} %first_ref.1, bf16[32,1152]{1,0:T(8,128)(2,1)} %second_ref.1, bf16[1,1152]{1,0:T(2,128)(2,1)} %broadcast_in_dim.3.gain_ref, f32[1,128]{1,0:T(1,128)} %constant.2.clone.freq_ref, bf16[1152,6656]{1,0:T(8,128)(2,1)} %qkv_ref.1, ...), custom_call_target="tpu_custom_call" | custom-call | tf_op jit(solution)/shard_map/pallas_call | solution.py:416
  51.7 1.5 %copy.13 = bf16[32,1152]{1,0:T(8,128)(2,1)} copy(bf16[32,1152]{1,0:T(8,128)(2,1)} %get-tuple-element.4) | data formatting | bytes 147456
  53.2 1.5 %copy.14 = bf16[32,1152]{1,0:T(8,128)(2,1)} copy(bf16[32,1152]{1,0:T(8,128)(2,1)} %get-tuple-element.5) | data formatting | bytes 147456

commit v2 on v1

--- a/solution.py
+++ b/solution.py
@@ -14,9 +14,16 @@
 HALF = HD // 2
 KV = 2 * HD
 
-GROUP = 8
-GROUPS = HEADS // GROUP
+SIZES = (8, 8, 8)
+STARTS = (0, 8, 16)
+GROUPS = len(SIZES)
 TILE = 512
+LOADS_A_STEP = 1
+
+SCHEDULE = (
+    (0, 0), (0, 1), (1, 0), (0, 2), (1, 1), (1, 2), (2, 0), (2, 1), (3, 0), (2, 2),
+    (3, 1), (4, 0), (3, 2), (4, 1), (5, 0), (4, 2), (5, 1), (6, 0), (5, 2), (6, 1), (6, 2),
+)
 
 eps_norm = 1e-05
 
@@ -33,8 +40,8 @@
 
 
 def chunk_columns(j):
-    width = GROUP * HD
-    return (0, KV + width) if j == 0 else (KV + j * width, width)
+    width = SIZES[j] * HD
+    return (0, KV + width) if j == 0 else (KV + STARTS[j] * HD, width)
 
 
 def kernel(
@@ -49,9 +56,12 @@
     cache_ref,
     lengths_ref,
     order_ref,
-    first_out_ref,
-    second_out_ref,
+    total,
     x,
+    gain,
+    freq,
+    lengths,
+    order,
     wq,
     wo,
     cache,
@@ -67,7 +77,6 @@
     gathered,
     spread,
     lhs,
-    total,
     in_sem,
     q_sem,
     o_sem,
@@ -101,38 +110,48 @@
     ahead = [lax.rem(hi + d, H) for d in range(H)]
     behind = [lax.rem(hi - d + H, H) for d in range(H)]
 
+    barrier = pltpu.get_barrier_semaphore()
+    partners = [lax.rem(me + d, n) for d in range(1, n)]
+    for partner in partners:
+        pl.semaphore_signal(
+            barrier, inc=1, device_id={"gx": partner}, device_id_type=pl.DeviceIdType.MESH
+        )
+
     loads = [
-        pltpu.make_async_copy(first_ref, x.at[pl.ds(0, R)], in_sem.at[0]),
-        pltpu.make_async_copy(second_ref, x.at[pl.ds(R, R)], in_sem.at[1]),
+        pltpu.make_async_copy(src, dst, in_sem.at[i])
+        for i, (src, dst) in enumerate(
+            [
+                (first_ref, x.at[pl.ds(0, R)]),
+                (second_ref, x.at[pl.ds(R, R)]),
+                (gain_ref, gain),
+                (freq_ref, freq),
+                (lengths_ref, lengths),
+                (order_ref, order),
+            ]
+        )
     ]
-    width = GROUP * HD
     kv_load = pltpu.make_async_copy(
         qkv_ref.at[:, pl.ds(HEADS * HD, KV)], wq.at[:, pl.ds(0, KV)], q_sem.at[GROUPS]
     )
     q_loads = [
         pltpu.make_async_copy(
-            qkv_ref.at[:, pl.ds(j * width, width)],
-            wq.at[:, pl.ds(KV + j * width, width)],
+            qkv_ref.at[:, pl.ds(start * HD, size * HD)],
+            wq.at[:, pl.ds(KV + start * HD, size * HD)],
             q_sem.at[j],
         )
-        for j in range(GROUPS)
+        for j, (start, size) in enumerate(zip(STARTS, SIZES))
     ]
-    cache_load = pltpu.make_async_copy(cache_ref, cache, in_sem.at[2])
+    cache_load = pltpu.make_async_copy(cache_ref, cache, in_sem.at[6])
     o_loads = [
         pltpu.make_async_copy(
-            out_w_ref.at[pl.ds(j * width, width)], wo.at[pl.ds(j * width, width)], o_sem.at[j]
-        )
-        for j in range(GROUPS)
+            out_w_ref.at[pl.ds(start * HD, size * HD)],
+            wo.at[pl.ds(start * HD, size * HD)],
+            o_sem.at[j],
+        )
+        for j, (start, size) in enumerate(zip(STARTS, SIZES))
     ]
-    for copy in loads + [kv_load] + q_loads + [cache_load] + o_loads:
+    for copy in loads + [kv_load, q_loads[0]]:
         copy.start()
-
-    barrier = pltpu.get_barrier_semaphore()
-    partners = [sibling, across] + [index_of(ahead[d], mid, core) for d in range(1, H)]
-    for partner in partners:
-        pl.semaphore_signal(
-            barrier, inc=1, device_id={"gx": partner}, device_id_type=pl.DeviceIdType.MESH
-        )
 
     sent = []
 
@@ -159,19 +178,22 @@
     sums = dot_nt(jnp.ones((8, features), BF16), rows)
     squares = jnp.sum(jnp.where(diagonal, dot_nt(rows, rows), 0.0), axis=0, keepdims=True)
     line = lax.broadcasted_iota(jnp.int32, (8, N), 0)
-    stat_own[...] = jnp.zeros_like(stat_own)
-    stat_own[0, :, :N] = jnp.where(line == 0, sums, jnp.broadcast_to(squares, (8, N)))
-
-    pl.semaphore_wait(barrier, len(partners))
-
-    copy = send(stat_own.at[0], stat_in.at[0], stat_send.at[0], stat_recv.at[0], sibling)
+    stat_own[...] = jnp.where(line == 0, sums, jnp.broadcast_to(squares, (8, N)))[:2]
+
+    pl.semaphore_wait(barrier, n - 1)
+    copies = [
+        send(stat_own, stat_in.at[d - 1], stat_send.at[d - 1], stat_recv.at[d - 1], partners[d - 1])
+        for d in range(1, n)
+    ]
+    for copy in [q_loads[1]]:
+        copy.start()
 
     lane = lax.broadcasted_iota(jnp.int32, (8, N), 1)
     holder = jnp.zeros((8, N), jnp.int32)
     for p in range(R):
         device, slot = p // slots, p % slots
         at = (((device % 2) * 2 + (device // 2) % 2) * H + device // 4) * slots + slot
-        holder = jnp.where(lane // 2 == at, order_ref[p], holder)
+        holder = jnp.where(lane // 2 == at, order[p], holder)
     holder = holder + (lane % 2) * R
     to_request = jnp.where(square == jnp.broadcast_to(holder[:1], (N, N)), 1.0, 0.0).astype(BF16)
     unit = jnp.where(diagonal, 1.0, 0.0).astype(BF16)
@@ -181,44 +203,28 @@
         row = lax.broadcasted_iota(jnp.int32, (count, HALF), 0)
         position = jnp.zeros((count, HALF), jnp.int32)
         for slot in range(slots):
-            position = jnp.where(row // (2 * per_row) == slot, lengths_ref[slot], position)
+            position = jnp.where(row // (2 * per_row) == slot, lengths[slot], position)
         position = position + (row // per_row) % 2
-        angles = position.astype(F32) * freq_ref[...]
+        angles = position.astype(F32) * freq[...]
         return jnp.cos(angles), jnp.sin(angles)
 
-    q_cos, q_sin = rotation(rp * GROUP, GROUP)
-
-    copy.wait_recv()
-    stat_own[1] = stat_own[0] + stat_in[0]
-    copy = send(stat_own.at[1], stat_in.at[1], stat_send.at[1], stat_recv.at[1], across)
-    k_cos, k_sin = rotation(rp, 1)
-    copy.wait_recv()
-    stat_own[2] = stat_own[1] + stat_in[1]
-    copies = [
-        send(
-            stat_own.at[2],
-            stat_in.at[1 + d],
-            stat_send.at[1 + d],
-            stat_recv.at[1 + d],
-            index_of(ahead[d], mid, core),
-        )
-        for d in range(1, H)
-    ]
-    for copy in copies:
-        copy.wait_recv()
-    stats = stat_own[2]
-    for d in range(1, H):
-        stats = stats + stat_in[1 + d]
+    turns = {size: rotation(rp * size, size) for size in set(SIZES) | {1}}
+    k_cos, k_sin = turns[1]
+
+    stats = stat_own[...]
+    for d in range(1, n):
+        copies[d - 1].wait_recv()
+        stats = stats + stat_in[d - 1]
 
     def as_column(row):
         return jnp.sum(
             jnp.where(diagonal, jnp.broadcast_to(row, (N, N)), 0.0), axis=1, keepdims=True
         )
 
-    mean = as_column(stats[0:1, :N]) / D
-    variance = as_column(stats[1:2, :N]) / D - mean * mean
+    mean = as_column(stats[0:1]) / D
+    variance = as_column(stats[1:2]) / D - mean * mean
     scaled = (rows.astype(F32) - mean) * lax.rsqrt(variance + eps_norm)
-    by_request = (scaled * gain_ref[...].astype(F32)).astype(BF16)
+    by_request = (scaled * gain[...].astype(F32)[None]).astype(BF16)
     normed[...] = dot_nn(to_slot, by_request).astype(BF16)
 
     def project(j):
@@ -283,6 +289,8 @@
 
     def attend(j, copies):
         start, count = chunk_columns(j)
+        size = SIZES[j]
+        q_cos, q_sin = turns[size]
         at = pl.ds(start, count)
         for copy in copies:
             copy.wait_recv()
@@ -301,23 +309,23 @@
                 padded = jnp.where(at_row == 0, one, jnp.where(at_row == 1, two, 0.0))
                 new_kv[slot] = padded.astype(BF16)
             cache_load.wait()
-        for h in range(GROUP):
+        for h in range(size):
             for part in range(2):
                 begin = q_start + h * HD + part * HALF
-                query[part, pl.ds(h, rp, stride=GROUP), :] = rows[:, begin : begin + HALF]
-        queries = turn(query[0], query[1], q_cos, q_sin)
+                query[part, pl.ds(h, rp, stride=size), :] = rows[:, begin : begin + HALF]
+        queries = turn(query[0, : rp * size], query[1, : rp * size], q_cos, q_sin)
         scale = HD ** (-0.5)
         context = cache.shape[1]
-        span = 2 * GROUP
+        span = 2 * size
         lane_old = lax.broadcasted_iota(jnp.int32, (span, context), 1)
         lane_new = lax.broadcasted_iota(jnp.int32, (span, 128), 1)
-        step = lax.broadcasted_iota(jnp.int32, (span, 128), 0) // GROUP
+        step = lax.broadcasted_iota(jnp.int32, (span, 128), 0) // size
         results = []
         for slot in range(slots):
             q = queries[slot * span : (slot + 1) * span].astype(BF16)
             old = dot_nt(q, cache[slot, :, :HD]) * scale
             new = dot_nt(q, new_kv[slot, :, :HD]) * scale
-            old = jnp.where(lane_old < lengths_ref[slot], old, -jnp.inf)
+            old = jnp.where(lane_old < lengths[slot], old, -jnp.inf)
             new = jnp.where(lane_new <= step, new, -jnp.inf)
             peak = jnp.maximum(
                 jnp.max(old, axis=1, keepdims=True), jnp.max(new, axis=1, keepdims=True)
@@ -330,8 +338,8 @@
             weighted = dot_nn(old.astype(BF16), cache[slot, :, HD:])
             weighted = weighted + dot_nn(new.astype(BF16), new_kv[slot, :, HD:])
             results.append(weighted / denominator)
-        gathered[j, core, mid, hi] = jnp.concatenate(results, axis=0).astype(BF16)
-        block = gathered.at[j, core, mid, hi]
+        gathered[j][core, mid, hi] = jnp.concatenate(results, axis=0).astype(BF16)
+        block = gathered[j].at[core, mid, hi]
         return [
             send(
                 block,
@@ -346,56 +354,44 @@
     def pass_mid(j, copies):
         for copy in copies:
             copy.wait_recv()
-        block = gathered.at[j, core, mid]
+        block = gathered[j].at[core, mid]
         return send(block, block, gmid_send.at[j], gmid_recv.at[j], across)
 
     def pass_core(j, copy):
         copy.wait_recv()
-        block = gathered.at[j, core]
+        block = gathered[j].at[core]
         return send(block, block, gcore_send.at[j], gcore_recv.at[j], sibling)
 
     def mix(j, copy):
         copy.wait_recv()
         o_loads[j].wait()
-        everything = gathered[j].reshape(N * GROUP, HD).astype(F32)
-        spread[0] = everything[:, :HALF]
-        spread[1] = everything[:, HALF:]
-        for h in range(GROUP):
+        size = SIZES[j]
+        width = size * HD
+        first_row = STARTS[j] * HD
+        everything = gathered[j][...].reshape(N * size, HD).astype(F32)
+        spread[0, : N * size] = everything[:, :HALF]
+        spread[1, : N * size] = everything[:, HALF:]
+        for h in range(size):
             head = jnp.concatenate(
-                [spread[part, pl.ds(h, N, stride=GROUP), :] for part in range(2)], axis=1
+                [spread[part, pl.ds(h, N, stride=size), :] for part in range(2)], axis=1
             ).astype(BF16)
             lhs[:, h * HD : (h + 1) * HD] = dot_nn(to_request, head).astype(BF16)
 
         for k in range(0, width, 512):
-            product = dot_nn(lhs[:, k : k + 512], wo[j * width + k : j * width + k + 512, :])
+            product = dot_nn(lhs[:, k : k + 512], wo[first_row + k : first_row + k + 512, :])
             if j == 0 and k == 0:
                 total[...] = product
             else:
                 total[...] += product
 
-    a0 = project(0)
-    a1 = project(1)
-    b0 = add_core(0, a0)
-    a2 = project(2)
-    b1 = add_core(1, a1)
-    b2 = add_core(2, a2)
-    c0 = add_mid(0, b0)
-    c1 = add_mid(1, b1)
-    g0 = attend(0, c0)
-    c2 = add_mid(2, b2)
-    g1 = attend(1, c1)
-    g0 = pass_mid(0, g0)
-    g2 = attend(2, c2)
-    g1 = pass_mid(1, g1)
-    g0 = pass_core(0, g0)
-    g2 = pass_mid(2, g2)
-    g1 = pass_core(1, g1)
-    mix(0, g0)
-    g2 = pass_core(2, g2)
-    mix(1, g1)
-    mix(2, g2)
-    first_out_ref[...] = (x[:R].astype(F32) + total[:R]).astype(BF16)
-    second_out_ref[...] = (x[R:].astype(F32) + total[R:]).astype(BF16)
+    held = [None] * GROUPS
+    steps = (project, add_core, add_mid, attend, pass_mid, pass_core, mix)
+    later = q_loads[2:] + [cache_load] + o_loads
+    for stage, j in SCHEDULE:
+        for copy in later[:LOADS_A_STEP]:
+            copy.start()
+        later = later[LOADS_A_STEP:]
+        held[j] = project(j) if stage == 0 else steps[stage](j, held[j])
     for copy in sent:
         copy.wait_send()
 
@@ -407,40 +403,41 @@
     slots, context, _ = kv_cache.shape
     N, rp, H = 2 * R, 2 * slots, n // 4
     columns = qkv_weight.shape[1]
-    lanes = max(N, 128)
     frequencies = (10000.0 ** (-np.arange(HALF) / HALF)).astype(np.float32)[None]
     anywhere = pl.BlockSpec(memory_space=pl.ANY)
     vmem = pl.BlockSpec(memory_space=pltpu.VMEM)
-    smem = pl.BlockSpec(memory_space=pltpu.SMEM)
     dma = pltpu.SemaphoreType.DMA
-    return pl.pallas_call(
+    mixed = pl.pallas_call(
         functools.partial(kernel, n, slots),
-        out_shape=[jax.ShapeDtypeStruct((R, features), BF16)] * 2,
-        in_specs=[anywhere, anywhere, vmem, vmem, anywhere, anywhere, anywhere, smem, smem],
-        out_specs=[vmem, vmem],
+        out_shape=jax.ShapeDtypeStruct((N, features), F32),
+        in_specs=[anywhere] * 9,
+        out_specs=vmem,
         scratch_shapes=[
             pltpu.VMEM((N, features), BF16),
+            pltpu.VMEM((features,), BF16),
+            pltpu.VMEM((1, HALF), F32),
+            pltpu.SMEM((slots,), jnp.int32),
+            pltpu.SMEM((R,), jnp.int32),
             pltpu.VMEM((features, columns), BF16),
             pltpu.VMEM((HEADS * HD, features), BF16),
             pltpu.VMEM((slots, context, KV), BF16),
-            pltpu.VMEM((3, 8, lanes), F32),
-            pltpu.VMEM((H + 1, 8, lanes), F32),
+            pltpu.VMEM((2, N), F32),
+            pltpu.VMEM((n - 1, 2, N), F32),
             pltpu.VMEM((N, features), BF16),
             pltpu.VMEM((2, 2, H, rp, columns), F32),
             pltpu.VMEM((2, H, rp, columns), F32),
             pltpu.VMEM((H, rp, columns), F32),
             pltpu.VMEM((H - 1, rp, columns), F32),
-            pltpu.VMEM((2, rp * GROUP, HALF), F32),
+            pltpu.VMEM((2, rp * max(SIZES), HALF), F32),
             pltpu.VMEM((slots, 128, KV), BF16),
-            pltpu.VMEM((GROUPS, 2, 2, H, rp * GROUP, HD), BF16),
-            pltpu.VMEM((2, N * GROUP, HALF), F32),
-            pltpu.VMEM((N, GROUP * HD), BF16),
-            pltpu.VMEM((N, features), F32),
-            dma((3,)),
+            tuple(pltpu.VMEM((2, 2, H, rp * size, HD), BF16) for size in SIZES),
+            pltpu.VMEM((2, N * max(SIZES), HALF), F32),
+            pltpu.VMEM((N, max(SIZES) * HD), BF16),
+            dma((7,)),
             dma((GROUPS + 1,)),
             dma((GROUPS,)),
-            dma((H + 1,)),
-            dma((H + 1,)),
+            dma((n - 1,)),
+            dma((n - 1,)),
             dma((GROUPS,)),
             dma((GROUPS,)),
             dma((GROUPS,)),
@@ -460,7 +457,7 @@
     )(
         first_tokens,
         second_tokens,
-        ln_gain[None],
+        ln_gain,
         jnp.asarray(frequencies),
         qkv_weight,
         out_weight,
@@ -468,6 +465,9 @@
         lengths,
         order,
     )
+    first_out = (first_tokens.astype(F32) + mixed[:R]).astype(BF16)
+    second_out = (second_tokens.astype(F32) + mixed[R:]).astype(BF16)
+    return first_out, second_out
 
 
 def solution(mesh):

time: 55 us -> 45.6 us (0.83)
  Pallas kernels: 49.8 us -> 43.1 us
  local copies, waits for them, and re-layouts: 4.33 us -> 0.01 us
  other arithmetic: 0 us -> 1.67 us
    pallas_call x1, Pallas kernels: 49.8 us -> 43.1 us  [on_device(): pl.pallas_call(functools.partial(kernel, n, slots), out_shape=jax.ShapeDt...]
    unnamed x2 -> x4, local copies, waits for them, and re-layouts: 3.04 us -> 0.01 us
    convert_element_type x0 -> x1, other arithmetic: none -> 1.67 us  [on_device(): second_out = (second_tokens.astype(F32) + mixed[R:]).astype(BF16)]
    broadcast_in_dim x1 -> x0, local copies, waits for them, and re-layouts: 1.28 us -> none  [on_device(): ln_gain[None]]
where the time goes in v2:
time: 45.6 us; the launch traced here: 45.5 us
  Pallas kernels  43.1 us (95%)
  other arithmetic  1.67 us (4%)
  between operations  0.67 us (1%)
    pallas_call x1, Pallas kernels, on_device(): pl.pallas_call(functools.partial(kernel, n, slots), out_shape=jax.ShapeDt...  43.1 us
    convert_element_type x1, other arithmetic, on_device(): second_out = (second_tokens.astype(F32) + mixed[R:]).astype(BF16)  1.67 us

profile of v2, /device:TPU:0, one launch (start us, length us, event | category | flops | bytes accessed | tf_op | source)
XLA Modules:
  0.0 45.5 jit_solution(6028243124146277358)
XLA Ops:
  0.6 0.0 copy-start.1
  0.6 0.0 copy-start
  0.7 43.1 %shard_map.104 = f32[64,1152]{1,0:T(8,128)} custom-call(bf16[32,1152]{1,0:T(8,128)(2,1)} %first_ref.1, bf16[32,1152]{1,0:T(8,128)(2,1)} %second_ref.1, bf16[1152]{0:T(1024)(128)(2,1)} %gain_ref.1, f32[1,128]{1,0:T(1,128)} %constant.2.clone.freq_ref, bf16[1152,6656]{1,0:T(8,128)(2,1)} %qkv_ref.1, bf16[6144,1152]{1,0:T(8,128)(2,1)} %out_w_ref.1, ...), custom_call_target="tpu_custom_call" | custom-call | tf_op jit(solution)/shard_map/pallas_call | solution.py:410
  43.8 0.0 copy-done.1
  43.8 0.0 copy-done
  43.8 1.7 %add_convert_fusion = (bf16[32,1152]{1,0:T(8,128)(2,1)}, bf16[32,1152]{1,0:T(8,128)(2,1)}) fusion(f32[64,1152]{1,0:T(8,128)} %shard_map.104, bf16[32,1152]{1,0:T(8,128)(2,1)S(1)} %copy-done.1, bf16[32,1152]{1,0:T(8,128)(2,1)S(1)} %copy-done), kind=kLoop, calls=%fused_computation | loop fusion | flops 221184 | bytes 589824 | tf_op jit(solution)/shard_map/convert_element_type | solution.py:469
Async XLA Ops:
  0.6 43.2 %copy-start.1 = (bf16[32,1152]{1,0:T(8,128)(2,1)S(1)}, bf16[32,1152]{1,0:T(8,128)(2,1)}, u32[]{:S(2)}) copy-start(bf16[32,1152]{1,0:T(8,128)(2,1)} %second_ref.1) | copy-start | bytes 221188
  0.6 43.2 %copy-start = (bf16[32,1152]{1,0:T(8,128)(2,1)S(1)}, bf16[32,1152]{1,0:T(8,128)(2,1)}, u32[]{:S(2)}) copy-start(bf16[32,1152]{1,0:T(8,128)(2,1)} %first_ref.1) | copy-start | bytes 221188

commit v3 on v2

--- a/solution.py
+++ b/solution.py
@@ -21,8 +21,9 @@
 LOADS_A_STEP = 1
 
 SCHEDULE = (
-    (0, 0), (0, 1), (1, 0), (0, 2), (1, 1), (1, 2), (2, 0), (2, 1), (3, 0), (2, 2),
-    (3, 1), (4, 0), (3, 2), (4, 1), (5, 0), (4, 2), (5, 1), (6, 0), (5, 2), (6, 1), (6, 2),
+    (0, 0), (0, 1), (1, 0), (0, 2), (1, 1), (0, 3), (1, 2), (0, 4), (2, 0), (1, 3), (1, 4),
+    (2, 1), (2, 2), (3, 0), (2, 3), (2, 4), (3, 1), (4, 0), (3, 2), (4, 1), (5, 0), (4, 2),
+    (5, 1), (6, 0), (6, 1), (6, 2),
 )
 
 eps_norm = 1e-05
@@ -39,9 +40,13 @@
     return jnp.dot(a, b, preferred_element_type=F32)
 
 
-def chunk_columns(j):
-    width = SIZES[j] * HD
-    return (0, KV + width) if j == 0 else (KV + STARTS[j] * HD, width)
+PIECES = (
+    (0, 1536, 0),
+    (1536, 1024, 0),
+    (2560, 2048, 1),
+    (4608, 1024, 2),
+    (5632, 1024, 2),
+)
 
 
 def kernel(
@@ -94,6 +99,8 @@
     gmid_recv,
     gcore_send,
     gcore_recv,
+    row_send,
+    row_recv,
 ):
     H = n // 4
     R = order_ref.shape[0]
@@ -228,10 +235,11 @@
     normed[...] = dot_nn(to_slot, by_request).astype(BF16)
 
     def project(j):
-        start, count = chunk_columns(j)
+        start, count, group = PIECES[j]
         if j == 0:
             kv_load.wait()
-        q_loads[j].wait()
+        if j == 0 or PIECES[j - 1][2] != group:
+            q_loads[group].wait()
 
         @pl.loop(0, count // TILE)
         def _(i):
@@ -252,7 +260,7 @@
         )
 
     def add_core(j, copy):
-        start, count = chunk_columns(j)
+        start, count, _ = PIECES[j]
         at = pl.ds(start, count)
         copy.wait_recv()
         from_core[1 - mid, :, :, at] = from_core[1 - mid, :, :, at] + partial[core, 1 - mid, :, :, at]
@@ -267,7 +275,7 @@
         return copy
 
     def add_mid(j, copy):
-        start, count = chunk_columns(j)
+        start, count, _ = PIECES[j]
         at = pl.ds(start, count)
         copy.wait_recv()
         from_mid[:, :, at] = from_mid[:, :, at] + from_core[mid, :, :, at]
@@ -288,7 +296,8 @@
         )
 
     def attend(j, copies):
-        start, count = chunk_columns(j)
+        start = min(first for first, _, group in PIECES if group == j)
+        count = sum(columns for _, columns, group in PIECES if group == j)
         size = SIZES[j]
         q_cos, q_sin = turns[size]
         at = pl.ds(start, count)
@@ -355,15 +364,23 @@
         for copy in copies:
             copy.wait_recv()
         block = gathered[j].at[core, mid]
-        return send(block, block, gmid_send.at[j], gmid_recv.at[j], across)
+        copy = send(block, block, gmid_send.at[j], gmid_recv.at[j], across)
+        if j < GROUPS - 1:
+            return copy
+        others = [index_of(hi, mid, 1 - core), index_of(hi, 1 - mid, 1 - core)]
+        return [copy] + [
+            send(block, block, row_send.at[k], row_recv.at[k], partner)
+            for k, partner in enumerate(others)
+        ]
 
     def pass_core(j, copy):
         copy.wait_recv()
         block = gathered[j].at[core]
         return send(block, block, gcore_send.at[j], gcore_recv.at[j], sibling)
 
-    def mix(j, copy):
-        copy.wait_recv()
+    def mix(j, copies):
+        for copy in copies if j == GROUPS - 1 else [copies]:
+            copy.wait_recv()
         o_loads[j].wait()
         size = SIZES[j]
         width = size * HD
@@ -385,13 +402,22 @@
                 total[...] += product
 
     held = [None] * GROUPS
+    summed = [None] * len(PIECES)
     steps = (project, add_core, add_mid, attend, pass_mid, pass_core, mix)
     later = q_loads[2:] + [cache_load] + o_loads
     for stage, j in SCHEDULE:
         for copy in later[:LOADS_A_STEP]:
             copy.start()
         later = later[LOADS_A_STEP:]
-        held[j] = project(j) if stage == 0 else steps[stage](j, held[j])
+        if stage == 0:
+            summed[j] = project(j)
+        elif stage < 3:
+            summed[j] = steps[stage](j, summed[j])
+        elif stage == 3:
+            pieces = [copies for copies, piece in zip(summed, PIECES) if piece[2] == j]
+            held[j] = attend(j, [copy for copies in pieces for copy in copies])
+        else:
+            held[j] = steps[stage](j, held[j])
     for copy in sent:
         copy.wait_send()
 
@@ -438,18 +464,20 @@
             dma((GROUPS,)),
             dma((n - 1,)),
             dma((n - 1,)),
-            dma((GROUPS,)),
-            dma((GROUPS,)),
-            dma((GROUPS,)),
-            dma((GROUPS,)),
-            dma((GROUPS, H - 1)),
-            dma((GROUPS, H - 1)),
+            dma((len(PIECES),)),
+            dma((len(PIECES),)),
+            dma((len(PIECES),)),
+            dma((len(PIECES),)),
+            dma((len(PIECES), H - 1)),
+            dma((len(PIECES), H - 1)),
             dma((GROUPS, H - 1)),
             dma((GROUPS, H - 1)),
             dma((GROUPS,)),
             dma((GROUPS,)),
             dma((GROUPS,)),
             dma((GROUPS,)),
+            dma((2,)),
+            dma((2,)),
         ],
         compiler_params=pltpu.CompilerParams(
             collective_id=0, has_side_effects=True, vmem_limit_bytes=56 * 2**20

time: 45.6 us -> 43.3 us (0.950)
  Pallas kernels: 43.1 us -> 40.7 us
    pallas_call x1, Pallas kernels: 43.1 us -> 40.7 us  [on_device(): pl.pallas_call(functools.partial(kernel, n, slots), out_shape=jax.ShapeDt...]
where the time goes in v3:
time: 43.3 us; the launch traced here: 43.1 us
  Pallas kernels  40.7 us (94%)
  other arithmetic  1.67 us (4%)
  between operations  0.67 us (2%)
    pallas_call x1, Pallas kernels, on_device(): pl.pallas_call(functools.partial(kernel, n, slots), out_shape=jax.ShapeDt...  40.7 us
    convert_element_type x1, other arithmetic, on_device(): second_out = (second_tokens.astype(F32) + mixed[R:]).astype(BF16)  1.67 us

profile of v3, /device:TPU:0, one launch (start us, length us, event | category | flops | bytes accessed | tf_op | source)
XLA Modules:
  0.0 43.1 jit_solution(1758850567180741058)
XLA Ops:
  0.6 0.0 copy-start.1
  0.6 0.0 copy-start
  0.7 40.7 %shard_map.104 = f32[64,1152]{1,0:T(8,128)} custom-call(bf16[32,1152]{1,0:T(8,128)(2,1)} %first_ref.1, bf16[32,1152]{1,0:T(8,128)(2,1)} %second_ref.1, bf16[1152]{0:T(1024)(128)(2,1)} %gain_ref.1, f32[1,128]{1,0:T(1,128)} %constant.2.clone.freq_ref, bf16[1152,6656]{1,0:T(8,128)(2,1)} %qkv_ref.1, bf16[6144,1152]{1,0:T(8,128)(2,1)} %out_w_ref.1, ...), custom_call_target="tpu_custom_call" | custom-call | tf_op jit(solution)/shard_map/pallas_call | solution.py:436
  41.4 0.0 copy-done.1
  41.4 0.0 copy-done
  41.4 1.7 %add_convert_fusion = (bf16[32,1152]{1,0:T(8,128)(2,1)}, bf16[32,1152]{1,0:T(8,128)(2,1)}) fusion(f32[64,1152]{1,0:T(8,128)} %shard_map.104, bf16[32,1152]{1,0:T(8,128)(2,1)S(1)} %copy-done.1, bf16[32,1152]{1,0:T(8,128)(2,1)S(1)} %copy-done), kind=kLoop, calls=%fused_computation | loop fusion | flops 221184 | bytes 589824 | tf_op jit(solution)/shard_map/convert_element_type | solution.py:497
Async XLA Ops:
  0.6 40.7 %copy-start.1 = (bf16[32,1152]{1,0:T(8,128)(2,1)S(1)}, bf16[32,1152]{1,0:T(8,128)(2,1)}, u32[]{:S(2)}) copy-start(bf16[32,1152]{1,0:T(8,128)(2,1)} %second_ref.1) | copy-start | bytes 221188
  0.6 40.7 %copy-start = (bf16[32,1152]{1,0:T(8,128)(2,1)S(1)}, bf16[32,1152]{1,0:T(8,128)(2,1)}, u32[]{:S(2)}) copy-start(bf16[32,1152]{1,0:T(8,128)(2,1)} %first_ref.1) | copy-start | bytes 221188
